TPU v7x, 32 devices: a whole 2x2x4 slice. The times are simulated.
32 devices in a mesh: dom: 16 (over z, x, core), snap: 2 (over y).
Axes of the slice: x: 2, y: 2, z: 4, core: 2. Of those that a mesh axis runs over, the one named last changes fastest.
Arguments:
- features: bfloat16 [8, 2048, 256], P('snap', 'dom'), may hold values from -6 to 6
- cotangent: bfloat16 [8, 2048, 256], P('snap', 'dom'), may hold values from -6 to 6
- neighbours: int32 [2048, 16], P('dom'), may hold values from 0 to 2047, as said below
- degrees: int32 [2048], P('dom'), may hold values from 1 to 16
- message_proj: bfloat16 [256, 256], replicated, may hold values from -0.375 to 0.375
- combine_proj: bfloat16 [256, 256], replicated, may hold values from -0.375 to 0.375
- attend_proj: bfloat16 [256, 768], replicated, may hold values from -0.375 to 0.375
- output_proj: bfloat16 [256, 256], replicated, may hold values from -0.375 to 0.375
Outputs:
- grad_features: bfloat16 [8, 2048, 256], P('snap', 'dom')
- grad_message: float32 [256, 256], replicated
- grad_combine: float32 [256, 256], replicated
- grad_attend: float32 [256, 768], replicated
- grad_output: float32 [256, 256], replicated
Inputs may be any that keep to these rules, and one draw needn't show every extreme that they name: `neighbours`: a neighbour of a node in rows p * 128 to (p + 1) * 128 - 1 lies in rows p * 128 - 128 to (p + 1) * 128 + 127; slot 0 of the first and of the second node of such a block names the lowest and the highest of those rows that exist.
All inputs are finite; a program needn't handle non-finite values.
Results may differ from a plain program's by a relative error of at most 0.012.
Values may be sent and summed in bfloat16 or wider, within the bound.
A program may use at most 64 MiB of HBM per device.

v0:
```python
import math

import jax
import jax.numpy as jnp
from jax import lax
from jax.sharding import PartitionSpec as P

HEAD_DIM = 32
SNAPS = 8
HALO = 128


def with_halo(cells, sides, width):
    for axis, dim in sides:
        count = lax.axis_size(axis)
        ends = count - 1
        head = lax.slice_in_dim(cells, 0, width, axis=dim)
        tail = lax.slice_in_dim(cells, cells.shape[dim] - width, cells.shape[dim], axis=dim)
        cells = jnp.concatenate(
            [
                lax.ppermute(tail, axis, [(i, (i + 1) % count) for i in range(ends)]),
                cells,
                lax.ppermute(head, axis, [((i + 1) % count, i) for i in range(ends)]),
            ],
            axis=dim,
        )
    return cells


def silu_slope(inputs_pre):
    logistic = jax.nn.sigmoid(inputs_pre)
    return logistic * (1.0 + inputs_pre * (1.0 - logistic))


def edge_inputs(message_rows, own_block, neighbour_block, degree_block):
    gathered = jnp.take(message_rows, neighbour_block, axis=0)
    before = gathered + own_block.astype(jnp.float32)[:, None, :]
    slot_index = jnp.arange(neighbour_block.shape[1], dtype=jnp.int32)
    used = (slot_index[None, :] < degree_block[:, None]).astype(jnp.float32)
    weights = used / degree_block.astype(jnp.float32)[:, None]
    return (before, weights)


def spatial_forward(own_rows, message_rows, neighbour_index, degrees, combine_proj, block_rows):
    node_count = own_rows.shape[0]

    def per_block(block_index):
        before, weights = edge_inputs(message_rows, own_rows, neighbour_index, degrees)
        return jnp.sum(jax.nn.silu(before) * weights[:, :, None], axis=1)

    combined = lax.map(per_block, jnp.arange(node_count // block_rows, dtype=jnp.int32))
    combined = combined.reshape(node_count, -1).astype(jnp.bfloat16)
    spatial = own_rows.astype(jnp.float32) + jnp.dot(
        combined, combine_proj, preferred_element_type=jnp.float32
    )
    return (combined, spatial.astype(jnp.bfloat16))


def spatial_backward(
    own_rows, message_rows, neighbour_index, degrees, grad_spatial, combine_proj, block_rows
):
    node_count = own_rows.shape[0]
    feature_width = own_rows.shape[1]
    grad_combined = jnp.dot(grad_spatial, combine_proj.T, preferred_element_type=jnp.float32)

    def per_block(totals, block_index):
        before, weights = edge_inputs(message_rows, own_rows, neighbour_index, degrees)
        grad_before = grad_combined[:, None, :] * weights[:, :, None] * silu_slope(before)
        totals = totals.at[neighbour_index.reshape(-1)].add(grad_before.reshape(-1, feature_width))
        return (totals, jnp.sum(grad_before, axis=1))

    start_rows = jnp.zeros((message_rows.shape[0], feature_width), jnp.float32)
    grad_rows, self_terms = lax.scan(
        per_block, start_rows, jnp.arange(node_count // block_rows, dtype=jnp.int32)
    )
    return (grad_rows, self_terms.reshape(node_count, feature_width))


def temporal_block(spat_block, cot_block, attend_proj, output_proj):
    snap_count, node_count, feature_width = spat_block.shape
    head_count = feature_width // HEAD_DIM
    row_count = snap_count * node_count
    flat_spat = spat_block.reshape(row_count, feature_width)
    flat_cot = cot_block.reshape(row_count, feature_width)
    projected = jnp.dot(flat_spat, attend_proj, preferred_element_type=jnp.float32)
    projected = projected.reshape(snap_count, node_count, 3, head_count, HEAD_DIM)
    query_rows = projected[:, :, 0]
    key_rows = projected[:, :, 1]
    value_rows = projected[:, :, 2]
    inverse_root = 1.0 / math.sqrt(HEAD_DIM)
    precise = lax.Precision.HIGHEST
    scores = jnp.einsum("snhe,rnhe->nhsr", query_rows, key_rows, precision=precise) * inverse_root
    exponent = jnp.exp(scores)
    soft_weights = exponent / jnp.sum(exponent, axis=-1, keepdims=True)
    attended = jnp.einsum("nhsr,rnhe->snhe", soft_weights, value_rows, precision=precise)
    attended = attended.reshape(row_count, feature_width).astype(jnp.bfloat16)
    grad_output = jnp.dot(attended.T, flat_cot, preferred_element_type=jnp.float32)
    grad_attended = jnp.dot(flat_cot, output_proj.T, preferred_element_type=jnp.float32)
    grad_attended = grad_attended.reshape(snap_count, node_count, head_count, HEAD_DIM)
    grad_soft = jnp.einsum("snhe,rnhe->nhsr", grad_attended, value_rows, precision=precise)
    grad_value = jnp.einsum("nhsr,snhe->rnhe", soft_weights, grad_attended, precision=precise)
    grad_score = (
        soft_weights
        * (grad_soft - jnp.sum(soft_weights * grad_soft, axis=-1, keepdims=True))
        * inverse_root
    )
    grad_query = jnp.einsum("nhsr,rnhe->snhe", grad_score, key_rows, precision=precise)
    grad_key = jnp.einsum("nhsr,snhe->rnhe", grad_score, query_rows, precision=precise)
    grad_three = jnp.stack([grad_query, grad_key, grad_value], axis=2)
    grad_three = grad_three.reshape(row_count, 3 * feature_width).astype(jnp.bfloat16)
    grad_attend = jnp.dot(flat_spat.T, grad_three, preferred_element_type=jnp.float32)
    grad_spatial = flat_cot.astype(jnp.float32) + jnp.dot(
        grad_three, attend_proj.T, preferred_element_type=jnp.float32
    )
    grad_spatial = grad_spatial.astype(jnp.bfloat16).reshape(snap_count, node_count, feature_width)
    return (grad_spatial, grad_attend, grad_output)


def body(
    features, cotangent, neighbours, degrees, message_proj, combine_proj, attend_proj, output_proj
):
    local_count, node_count, feature_width = features.shape
    block_rows = min(256, node_count)
    first_row = lax.axis_index("dom") * node_count - HALO
    neighbour_local = neighbours - first_row
    extended = with_halo(features, (("dom", 1),), HALO)
    message_list = []
    combined_list = []
    spatial_list = []
    for snapshot in range(local_count):
        message_rows = jnp.dot(extended[snapshot], message_proj, preferred_element_type=jnp.float32)
        combined, spatial = spatial_forward(
            features[snapshot], message_rows, neighbour_local, degrees, combine_proj, block_rows
        )
        message_list.append(message_rows)
        combined_list.append(combined)
        spatial_list.append(spatial)
    spatial_all = jnp.stack(spatial_list)
    spat_swapped, cot_swapped = (
        lax.all_to_all(spatial_all, "snap", split_axis=1, concat_axis=0, tiled=True),
        lax.all_to_all(cotangent, "snap", split_axis=1, concat_axis=0, tiled=True),
    )
    snap_count = spat_swapped.shape[0]
    node_share = spat_swapped.shape[1]
    node_block = min(128, node_share)

    def temporal_step(totals, block_index):
        grad_block, grad_attend, grad_output = temporal_block(
            spat_swapped, cot_swapped, attend_proj, output_proj
        )
        return ((totals[0] + grad_attend, totals[1] + grad_output, grad_block), None)

    start_totals = (
        jnp.zeros((feature_width, 3 * feature_width), jnp.float32),
        jnp.zeros((feature_width, feature_width), jnp.float32),
        jnp.zeros((snap_count, node_share, feature_width), jnp.bfloat16),
    )
    totals, unused_out = lax.scan(
        temporal_step, start_totals, jnp.arange(node_share // node_block, dtype=jnp.int32)
    )
    raw_attend, raw_output, grad_swapped = totals
    grad_spatial_all = lax.all_to_all(grad_swapped, "snap", split_axis=0, concat_axis=1, tiled=True)
    raw_combine = jnp.zeros((feature_width, feature_width), jnp.float32)
    grad_row_list = []
    self_list = []
    ghost_list = []
    for snapshot in range(local_count):
        grad_spatial = grad_spatial_all[snapshot]
        raw_combine = raw_combine + jnp.dot(
            combined_list[snapshot].T, grad_spatial, preferred_element_type=jnp.float32
        )
        grad_rows, self_terms = spatial_backward(
            features[snapshot],
            message_list[snapshot],
            neighbour_local,
            degrees,
            grad_spatial,
            combine_proj,
            block_rows,
        )
        grad_row_list.append(grad_rows)
        self_list.append(self_terms)
        ghost_list.append(
            jnp.concatenate([grad_rows[:HALO], grad_rows[node_count + HALO :]], axis=0)
        )
    returned = with_halo(jnp.stack(ghost_list).astype(jnp.bfloat16), (("dom", 1),), HALO).astype(
        jnp.float32
    )
    raw_message = jnp.zeros((feature_width, feature_width), jnp.float32)
    grad_list = []
    for snapshot in range(local_count):
        own_grads = grad_row_list[snapshot][HALO : HALO + node_count]
        own_grads = own_grads.at[:HALO].add(returned[snapshot, :HALO])
        own_grads = own_grads.at[node_count - HALO :].add(returned[snapshot, 3 * HALO :])
        own_grads = own_grads.astype(jnp.bfloat16)
        raw_message = raw_message + jnp.dot(
            features[snapshot].T, own_grads, preferred_element_type=jnp.float32
        )
        grad_here = grad_spatial_all[snapshot].astype(jnp.float32) + self_list[snapshot]
        grad_here = grad_here + jnp.dot(
            own_grads, message_proj.T, preferred_element_type=jnp.float32
        )
        grad_list.append(grad_here.astype(jnp.bfloat16))
    grad_features = jnp.stack(grad_list)
    raw_message, raw_combine, raw_attend, raw_output = lax.psum(
        (raw_message, raw_combine, raw_attend, raw_output), ("dom", "snap")
    )
    factor = 1.0 / math.sqrt(SNAPS * lax.axis_size("dom") * node_count)
    return (
        grad_features,
        raw_message * factor,
        raw_combine * factor,
        raw_attend * factor,
        raw_output * factor,
    )


def solution(mesh):
    in_specs = (
        P("snap", "dom", None),
        P("snap", "dom", None),
        P("dom", None),
        P("dom"),
        P(),
        P(),
        P(),
        P(),
    )
    out_specs = (P("snap", "dom", None), P(), P(), P(), P())
    return jax.shard_map(body, mesh=mesh, in_specs=in_specs, out_specs=out_specs, check_vma=False)
```

profile of v0, /device:TPU:0, one launch (start us, length us, event | category | flops | bytes accessed | tf_op | source)
XLA Modules:
  0.0 378.5 jit_solution(10846926036161951762)
XLA Ops:
  7.2 2.5 collective-permute-start
  12.9 3.6 all-to-all-start
  23.5 8.6 %gather_fusion = f32[2048,256]{1,0:T(8,128)} fusion(f32[384,256]{1,0:T(8,128)S(1)} %fusion.26, s32[2048]{0:T(1024)S(1)} %broadcast_clamp_fusion), kind=kCustom, calls=%fused_computation.clone | custom fusion | bytes 4202496 | tf_op jit(solution)/shard_map/while/body/eval_jaxpr/jit(_take)/gather | solution.py:36
  32.1 8.6 %gather_fusion.1 = f32[2048,256]{1,0:T(8,128)} fusion(f32[384,256]{1,0:T(8,128)S(1)} %fusion.25, s32[2048]{0:T(1024)S(1)} %broadcast_clamp_fusion), kind=kCustom, calls=%fused_computation.1.clone | custom fusion | bytes 4202496 | tf_op jit(solution)/shard_map/while/body/eval_jaxpr/jit(_take)/gather | solution.py:36
  40.6 8.5 %gather_fusion.2 = f32[2048,256]{1,0:T(8,128)} fusion(f32[384,256]{1,0:T(8,128)S(1)} %fusion.24, s32[2048]{0:T(1024)S(1)} %broadcast_clamp_fusion), kind=kCustom, calls=%fused_computation.2.clone | custom fusion | bytes 4202496 | tf_op jit(solution)/shard_map/while/body/eval_jaxpr/jit(_take)/gather | solution.py:36
  49.2 8.5 %gather_fusion.3 = f32[2048,256]{1,0:T(8,128)} fusion(f32[384,256]{1,0:T(8,128)S(1)} %fusion.23, s32[2048]{0:T(1024)S(1)} %broadcast_clamp_fusion), kind=kCustom, calls=%fused_computation.3.clone | custom fusion | bytes 4202496 | tf_op jit(solution)/shard_map/while/body/eval_jaxpr/jit(_take)/gather | solution.py:36
  57.8 5.8 %multiply_reduce_fusion.4 = (bf16[128,256]{1,0:T(8,128)(2,1)S(1)}, bf16[128,256]{1,0:T(8,128)(2,1)S(1)}, bf16[128,256]{1,0:T(8,128)(2,1)S(1)}, bf16[128,256]{1,0:T(8,128)(2,1)S(1)}) fusion(f32[2048,256]{1,0:T(8,128)S(1)} %copy-done.1, f32[128,16]{1,0:T(8,128)S(1)} %copy.147, f32[128,256]{1,0:T(8,128)S(1)} %get-tuple-element.411, ...), kind=kLoop, calls=%fused_computation.26 | loop fusion | flops 16646144 | bytes 9185280 | tf_op jit(solution)/shard_map/while/body/eval_jaxpr/reduce_sum | solution.py:49
  65.4 4.6 %all-to-all-start.1 = ((bf16[4,128,256]{2,0,1:T(4,128)(2,1)}), bf16[4,128,256]{2,0,1:T(4,128)(2,1)}, u32[]{:S(2)}, u32[]{:S(2)}) async-start(bf16[4,128,256]{2,0,1:T(4,128)(2,1)} %copy.154), calls=%async_computation.1 | async-start | bytes 524288 | tf_op jit(solution)/shard_map/all_to_all | solution.py:140
  71.3 2.9 copy.160
  80.9 4.1 %copy.158 = f32[8,64,8,32]{3,0,2,1:T(8,128)} copy(f32[8,64,8,32]{1,3,2,0:T(8,128)} %get-tuple-element.401) | data formatting | bytes 1048576 | tf_op jit(solution)/shard_map/while/body/eval_jaxpr/squeeze | solution.py:87
  85.0 4.0 %copy.162 = f32[8,64,8,32]{3,0,2,1:T(8,128)} copy(f32[8,64,8,32]{1,3,2,0:T(8,128)} %get-tuple-element.402) | data formatting | bytes 1048576 | tf_op jit(solution)/shard_map/while/body/eval_jaxpr/squeeze | solution.py:88
  89.1 2.8 copy.161
  91.9 6.5 %fusion.1 = (f32[64,8,8]{2,1,0:T(8,128)S(1)}, f32[64,8,8,8]{2,3,1,0:T(8,128)S(1)}) fusion(f32[8,64,8,32]{3,0,2,1:T(8,128)} %copy.158, f32[8,64,8,32]{3,0,2,1:T(8,128)} %copy.162), kind=kOutput, calls=%fused_computation.29 | convolution fusion | flops 12644352 | bytes 1196032 | tf_op jit(solution)/shard_map/while/body/eval_jaxpr/snhe,rnhe->nhsr/dot_general | solution.py:92
  98.4 5.6 %fusion.2 = bf16[8,64,8,32]{3,0,2,1:T(8,128)(2,1)} fusion(f32[8,64,8,32]{3,0,2,1:T(8,128)S(1)} %copy-done.11, f32[64,8,8,8]{2,3,1,0:T(8,128)S(1)} %get-tuple-element.428, f32[64,8,8]{2,1,0:T(8,128)S(1)} %get-tuple-element.427), kind=kOutput, calls=%fused_computation.31 | convolution fusion | flops 12779520 | bytes 933888 | tf_op jit(solution)/shard_map/while/body/eval_jaxpr/nhsr,rnhe->snhe/dot_general | solution.py:95
  104.0 4.4 %multiply_reduce_fusion = (f32[64,8,8]{2,1,0:T(8,128)S(1)}, f32[64,8,8,8]{2,3,1,0:T(8,128)S(1)}) fusion(f32[64,8,8]{2,1,0:T(8,128)S(1)} %get-tuple-element.427, f32[64,8,8,8]{2,3,1,0:T(8,128)S(1)} %get-tuple-element.428, f32[8,64,8,32]{3,0,2,1:T(8,128)S(1)} %copy-done.10, f32[8,64,8,32]{3,0,2,1:T(8,128)S(1)} %copy-done.11), kind=kOutput, calls=%fused_computation.18 | convolution fusion | flops 12709888 | bytes 1343488 | tf_op jit(solution)/shard_map/while/body/eval_jaxpr/snhe,rnhe->nhsr/dot_general | solution.py:100
  108.5 5.6 %fusion.22 = bf16[64,8,32,8]{2,3,1,0:T(8,128)(2,1)} fusion(f32[8,64,8,32]{3,0,2,1:T(8,128)S(1)} %copy-done.4, f32[64,8,8,8]{2,3,1,0:T(8,128)S(1)} %get-tuple-element.430, f32[64,8,8]{2,1,0:T(8,128)S(1)} %get-tuple-element.429, f32[64,8,8,8]{2,3,1,0:T(8,128)S(1)} %get-tuple-element.428, f32[64,8,8]{2,1,0:T(8,128)S(1)} %get-tuple-element.427), kind=kOutput, calls=%fused_computation.69 | convolution fusion | flops 12746752 | bytes 1081344 | tf_op jit(solution)/shard_map/while/body/eval_jaxpr/nhsr,rnhe->snhe/dot_general | solution.py:107
  114.1 5.4 %fusion.21 = bf16[64,8,32,8]{2,3,1,0:T(8,128)(2,1)} fusion(f32[8,64,8,32]{3,0,2,1:T(8,128)S(1)} %copy-done.3, f32[64,8,8,8]{2,3,1,0:T(8,128)S(1)} %get-tuple-element.430, f32[64,8,8]{2,1,0:T(8,128)S(1)} %get-tuple-element.429, f32[64,8,8,8]{2,3,1,0:T(8,128)S(1)} %get-tuple-element.428, f32[64,8,8]{2,1,0:T(8,128)S(1)} %get-tuple-element.427), kind=kOutput, calls=%fused_computation.68 | convolution fusion | flops 12746752 | bytes 1081344 | tf_op jit(solution)/shard_map/while/body/eval_jaxpr/nhsr,snhe->rnhe/dot_general | solution.py:108
  119.5 4.9 %fusion.69 = bf16[64,8,32,8]{2,3,1,0:T(8,128)(2,1)} fusion(f32[8,64,8,32]{3,0,2,1:T(8,128)S(1)} %copy-done.10, f32[64,8,8,8]{2,3,1,0:T(8,128)S(1)} %get-tuple-element.428, f32[64,8,8]{2,1,0:T(8,128)S(1)} %get-tuple-element.427), kind=kOutput, calls=%fused_computation.156 | convolution fusion | flops 12648448 | bytes 933888 | tf_op jit(solution)/shard_map/while/body/eval_jaxpr/nhsr,snhe->rnhe/dot_general | solution.py:101
  124.3 2.5 copy.179
  130.2 2.2 copy.166
  132.4 3.4 copy.168
  139.4 2.7 convert_element_type.200
  142.1 2.2 fusion.88
  146.5 3.4 all-to-all-start.2
  152.1 4.0 %all-to-all-done.2 = bf16[8,64,256]{2,1,0:T(8,128)(2,1)S(1)} async-done(((bf16[8,64,256]{2,1,0:T(8,128)(2,1)}), bf16[8,64,256]{2,1,0:T(8,128)(2,1)S(1)}, u32[]{:S(2)}, u32[]{:S(2)}) %all-to-all-start.2) | async-done | bytes 262176 | tf_op jit(solution)/shard_map/all_to_all | solution.py:162
  159.3 9.1 %fusion.72 = (f32[128,256]{1,0:T(8,128)}, f32[128,16,256]{2,1,0:T(8,128)}, f32[128,256]{1,0:T(8,128)}, f32[128,16,256]{2,1,0:T(8,128)}, f32[128,256]{1,0:T(8,128...) fusion(f32[128,256]{1,0:T(8,128)S(1)} %copy-done.16, pred[128,16]{1,0:T(8,128)(4,1)S(1)} %copy.145, ...), kind=kLoop, calls=%fused_computation.157 | loop fusion | flops 25034752 | bytes 18360320 | tf_op jit(solution)/shard_map/while/body/eval_jaxpr/reduce_sum | solution.py:70
  168.4 12.1 %scatter_custom_fusion = f32[384,256]{1,0:T(8,128)S(1)} fusion(s32[2048]{0:T(1024)} %bitcast.275, f32[2048,256]{1,0:T(8,128)} %bitcast.255, f32[]{:T(128)} %constant.390.clone.1), kind=kCustom, calls=%fused_computation.89 | custom fusion | flops 524288 | bytes 393728 | tf_op jit(solution)/shard_map/while/body/eval_jaxpr/scatter-add | solution.py:69
  180.5 12.2 %scatter_custom_fusion.1 = f32[384,256]{1,0:T(8,128)S(1)} fusion(s32[2048]{0:T(1024)} %bitcast.276, f32[2048,256]{1,0:T(8,128)} %bitcast.254, f32[]{:T(128)} %constant.390.clone.1), kind=kCustom, calls=%fused_computation.87 | custom fusion | flops 524288 | bytes 393728 | tf_op jit(solution)/shard_map/while/body/eval_jaxpr/scatter-add | solution.py:69
  192.8 12.1 %scatter_custom_fusion.2 = f32[384,256]{1,0:T(8,128)S(1)} fusion(s32[2048]{0:T(1024)} %bitcast.277, f32[2048,256]{1,0:T(8,128)} %bitcast.253, f32[]{:T(128)} %constant.390.clone.1), kind=kCustom, calls=%fused_computation.85 | custom fusion | flops 524288 | bytes 393728 | tf_op jit(solution)/shard_map/while/body/eval_jaxpr/scatter-add | solution.py:69
  205.0 12.1 %scatter_custom_fusion.3 = f32[384,256]{1,0:T(8,128)S(1)} fusion(s32[2048]{0:T(1024)} %bitcast.278, f32[2048,256]{1,0:T(8,128)} %bitcast.252, f32[]{:T(128)} %constant.390.clone.1), kind=kCustom, calls=%fused_computation.83 | custom fusion | flops 524288 | bytes 393728 | tf_op jit(solution)/shard_map/while/body/eval_jaxpr/scatter-add | solution.py:69
  221.5 4.0 %collective-permute-done.3 = bf16[4,128,256]{2,1,0:T(8,128)(2,1)S(1)} collective-permute-done((bf16[4,128,256]{2,1,0:T(8,128)(2,1)S(1)}, bf16[4,128,256]{2,1,0:T(8,128)(2,1)S(1)}, u32[]{:S(2)}, u32[]{:S(2)}) %collective-permute-start.3) | collective-permute-done | bytes 262176 | tf_op jit(solution)/shard_map/ppermute | solution.py:23
  228.9 137.0 %all-reduce.3.cloned.1.call-done = (f32[256,256]{0,1:T(8,128)}, f32[256,256]{0,1:T(8,128)}, f32[256,768]{1,0:T(8,128)}, f32[256,256]{0,1:T(8,128)}) async-done(((f32[256,256]{0,1:T(8,128)}, f32[256,256]{0,1:T(8,128)}, f32[256,768]{1,0:T(8,128)}, f32[256,256]{0,1:T(8,128)}), (f32[256,256]{0,1:T(8,128)}, f32[256,256]{0,1:T(8,128)}, f32[256,768]{1,0:T(8,128)}, ...) | async-done | bytes 1572880 | tf_op jit(solution)/shard_map/psum | solution.py:205
  (164 shorter events, 47.3 us)
Async XLA Ops:
  7.2 15.5 %copy-start = (bf16[256,256]{1,0:T(8,128)(2,1)S(1)}, bf16[256,256]{1,0:T(8,128)(2,1)}, u32[]{:S(2)}) copy-start(bf16[256,256]{1,0:T(8,128)(2,1)} %param.46) | copy-start | bytes 393220
  7.2 15.4 %copy-start.6 = (bf16[4,128,256]{2,1,0:T(8,128)(2,1)S(1)}, bf16[4,128,256]{2,1,0:T(8,128)(2,1)}, u32[]{:S(2)}) copy-start(bf16[4,128,256]{2,1,0:T(8,128)(2,1)} %param.42) | copy-start | bytes 786436
  7.2 12.1 %copy-start.35 = (s32[128]{0:T(128)S(1)}, s32[128]{0:T(128)}, u32[]{:S(2)}) copy-start(s32[128]{0:T(128)} %param.45) | copy-start | bytes 1540
  7.2 12.3 %copy-start.12 = (bf16[256,768]{1,0:T(8,128)(2,1)S(1)}, bf16[256,768]{1,0:T(8,128)(2,1)}, u32[]{:S(2)}) copy-start(bf16[256,768]{1,0:T(8,128)(2,1)} %param.48) | copy-start | bytes 1179652
  7.2 15.3 %collective-permute-start = (bf16[4,128,256]{2,1,0:T(8,128)(2,1)}, bf16[4,128,256]{2,1,0:T(8,128)(2,1)S(1)}, u32[]{:S(2)}, u32[]{:S(2)}) collective-permute-start(bf16[4,128,256]{2,1,0:T(8,128)(2,1)} %param.42), channel_id=1, source_target_pairs={{0,2},{2,4},{4,6},{6,8},{8,10},{10,12},{12,14},{14,16},{16,18},{18... | collective-permute-start | bytes 786440 | tf_op jit(solution)/shard_map/ppermute | solution.py:21
  9.7 12.9 %collective-permute-start.1 = (bf16[4,128,256]{2,1,0:T(8,128)(2,1)}, bf16[4,128,256]{2,1,0:T(8,128)(2,1)S(1)}, u32[]{:S(2)}, u32[]{:S(2)}) collective-permute-start(bf16[4,128,256]{2,1,0:T(8,128)(2,1)} %param.42), channel_id=1, source_target_pairs={{2,0},{4,2},{6,4},{8,6},{10,8},{12,10},{14,12},{16,14},{18,16},{20... | collective-permute-start | bytes 786440 | tf_op jit(solution)/shard_map/ppermute | solution.py:23
  12.9 8.9 %all-to-all-start = ((bf16[4,128,256]{2,0,1:T(4,128)(2,1)}), bf16[4,128,256]{2,0,1:T(4,128)(2,1)S(1)}, u32[]{:S(2)}, u32[]{:S(2)}) async-start(bf16[4,128,256]{2,0,1:T(4,128)(2,1)} %copy.143), calls=%async_computation | async-start | bytes 524288 | tf_op jit(solution)/shard_map/all_to_all | solution.py:141
  17.5 40.2 %copy-start.13 = (f32[128,256]{1,0:T(8,128)}, f32[128,256]{1,0:T(8,128)S(1)}, u32[]{:S(2)}) copy-start(f32[128,256]{1,0:T(8,128)S(1)} %get-tuple-element.410) | copy-start | bytes 393220
  17.5 40.2 %copy-start.15 = (f32[128,256]{1,0:T(8,128)}, f32[128,256]{1,0:T(8,128)S(1)}, u32[]{:S(2)}) copy-start(f32[128,256]{1,0:T(8,128)S(1)} %get-tuple-element.411) | copy-start | bytes 393220
  17.5 40.2 %copy-start.17 = (f32[128,256]{1,0:T(8,128)}, f32[128,256]{1,0:T(8,128)S(1)}, u32[]{:S(2)}) copy-start(f32[128,256]{1,0:T(8,128)S(1)} %get-tuple-element.412) | copy-start | bytes 393220
  19.5 38.2 %copy-start.23 = (f32[128,16]{1,0:T(8,128)}, f32[128,16]{1,0:T(8,128)S(1)}, u32[]{:S(2)}) copy-start(f32[128,16]{1,0:T(8,128)S(1)} %copy.147) | copy-start | bytes 24580
  49.2 8.6 %copy-start.1 = (f32[2048,256]{1,0:T(8,128)S(1)}, f32[2048,256]{1,0:T(8,128)}, u32[]{:S(2)}) copy-start(f32[2048,256]{1,0:T(8,128)} %gather_fusion) | copy-start | bytes 6291460
  57.7 5.8 %copy-start.5 = (bf16[256,256]{1,0:T(8,128)(2,1)S(1)}, bf16[256,256]{1,0:T(8,128)(2,1)}, u32[]{:S(2)}) copy-start(bf16[256,256]{1,0:T(8,128)(2,1)} %param.47) | copy-start | bytes 393220
  65.4 10.5 %all-to-all-start.1 = ((bf16[4,128,256]{2,0,1:T(4,128)(2,1)}), bf16[4,128,256]{2,0,1:T(4,128)(2,1)}, u32[]{:S(2)}, u32[]{:S(2)}) async-start(bf16[4,128,256]{2,0,1:T(4,128)(2,1)} %copy.154), calls=%async_computation.1 | async-start | bytes 524288 | tf_op jit(solution)/shard_map/all_to_all | solution.py:140
  91.9 6.5 %copy-start.11 = (f32[8,64,8,32]{3,0,2,1:T(8,128)S(1)}, f32[8,64,8,32]{3,0,2,1:T(8,128)}, u32[]{:S(2)}) copy-start(f32[8,64,8,32]{3,0,2,1:T(8,128)} %copy.161) | copy-start | bytes 1572868
  98.4 5.6 %copy-start.10 = (f32[8,64,8,32]{3,0,2,1:T(8,128)S(1)}, f32[8,64,8,32]{3,0,2,1:T(8,128)}, u32[]{:S(2)}) copy-start(f32[8,64,8,32]{3,0,2,1:T(8,128)} %copy.160) | copy-start | bytes 1572868
  104.0 4.5 %copy-start.4 = (f32[8,64,8,32]{3,0,2,1:T(8,128)S(1)}, f32[8,64,8,32]{3,0,2,1:T(8,128)}, u32[]{:S(2)}) copy-start(f32[8,64,8,32]{3,0,2,1:T(8,128)} %copy.162) | copy-start | bytes 1572868
  108.5 5.6 %copy-start.3 = (f32[8,64,8,32]{3,0,2,1:T(8,128)S(1)}, f32[8,64,8,32]{3,0,2,1:T(8,128)}, u32[]{:S(2)}) copy-start(f32[8,64,8,32]{3,0,2,1:T(8,128)} %copy.158) | copy-start | bytes 1572868
  139.4 5.0 %copy-start.8 = (bf16[4,2,64,256]{3,2,0,1:T(8,128)(2,1)S(1)}, bf16[4,2,64,256]{3,2,0,1:T(8,128)(2,1)}, u32[]{:S(2)}) copy-start(bf16[4,2,64,256]{3,2,0,1:T(8,128)(2,1)} %copy.144) | copy-start | bytes 786436
  146.5 9.6 %all-to-all-start.2 = ((bf16[8,64,256]{2,1,0:T(8,128)(2,1)}), bf16[8,64,256]{2,1,0:T(8,128)(2,1)S(1)}, u32[]{:S(2)}, u32[]{:S(2)}) async-start(bf16[8,64,256]{2,1,0:T(8,128)(2,1)} %bitcast.270), calls=%async_computation.2 | async-start | bytes 524288 | tf_op jit(solution)/shard_map/all_to_all | solution.py:162
  149.9 9.3 %copy-start.14 = (f32[128,256]{1,0:T(8,128)S(1)}, f32[128,256]{1,0:T(8,128)}, u32[]{:S(2)}) copy-start(f32[128,256]{1,0:T(8,128)} %copy-done.13) | copy-start | bytes 393220
  149.9 9.3 %copy-start.16 = (f32[128,256]{1,0:T(8,128)S(1)}, f32[128,256]{1,0:T(8,128)}, u32[]{:S(2)}) copy-start(f32[128,256]{1,0:T(8,128)} %copy-done.15) | copy-start | bytes 393220
  150.0 9.3 %copy-start.18 = (f32[128,256]{1,0:T(8,128)S(1)}, f32[128,256]{1,0:T(8,128)}, u32[]{:S(2)}) copy-start(f32[128,256]{1,0:T(8,128)} %copy-done.17) | copy-start | bytes 393220
  150.0 215.9 %all-reduce.3.cloned.1.call-start = ((), (), s32[]{:S(2)}) async-start(), calls=%async_computation.3 | async-start | bytes 3145728 | tf_op jit(solution)/shard_map/psum | solution.py:205
  156.1 3.2 copy-start.2
  217.0 3.3 copy-start.27
  217.1 3.5 copy-start.25
  217.2 8.3 %copy-start.7 = (bf16[4,128,256]{2,1,0:T(8,128)(2,1)S(1)}, bf16[4,128,256]{2,1,0:T(8,128)(2,1)}, u32[]{:S(2)}) copy-start(bf16[4,128,256]{2,1,0:T(8,128)(2,1)} %param.42) | copy-start | bytes 786436
  217.3 4.2 %collective-permute-start.2 = (bf16[4,128,256]{2,1,0:T(8,128)(2,1)S(1)}, bf16[4,128,256]{2,1,0:T(8,128)(2,1)S(1)}, u32[]{:S(2)}, u32[]{:S(2)}) collective-permute-start(bf16[4,128,256]{2,1,0:T(8,128)(2,1)S(1)} %get-tuple-element.403), channel_id=1, source_target_pairs={{0,2},{2,4},{4,6},{6,8},{8,10},{10,12},{12,14},{14,16},{16,18},{18... | collective-permute-start | bytes 786440 | tf_op jit(solution)/shard_map/ppermute | solution.py:21
  219.0 6.5 %collective-permute-start.3 = (bf16[4,128,256]{2,1,0:T(8,128)(2,1)S(1)}, bf16[4,128,256]{2,1,0:T(8,128)(2,1)S(1)}, u32[]{:S(2)}, u32[]{:S(2)}) collective-permute-start(bf16[4,128,256]{2,1,0:T(8,128)(2,1)S(1)} %get-tuple-element.404), channel_id=1, source_target_pairs={{2,0},{4,2},{6,4},{8,6},{10,8},{12,10},{14,12},{16,14},{18,16},{20... | collective-permute-start | bytes 786440 | tf_op jit(solution)/shard_map/ppermute | solution.py:23
  365.8 3.9 %copy-start.34 = (f32[256,256]{0,1:T(8,128)S(1)}, f32[256,256]{0,1:T(8,128)}, u32[]{:S(2)}) copy-start(f32[256,256]{0,1:T(8,128)} %get-tuple-element.387) | copy-start | bytes 786436
  365.8 4.8 %copy-start.33 = (f32[256,256]{0,1:T(8,128)S(1)}, f32[256,256]{0,1:T(8,128)}, u32[]{:S(2)}) copy-start(f32[256,256]{0,1:T(8,128)} %get-tuple-element.389) | copy-start | bytes 786436
  (12 other events, 13.8 us)
Sparse Core Ops, SparseCore 0:
  227.4 138.4 all-reduce.2
where the time goes:
time: 383 us; the launch traced here: 379 us
  waiting for transfers between devices  148 us (39%)
  local copies, waits for them, and re-layouts  75.8 us (20%)
  other arithmetic  71.3 us (19%)
  matrix products  49.7 us (13%)
  starting transfers between devices  18.5 us (5%)
  between operations  15.1 us (4%)
    psum x1, waiting for transfers between devices, body(): lax.psum((raw_message, raw_combine, raw_attend, raw_output), ('dom', 'sna...  137 us
    scatter-add x4, other arithmetic, per_block(): totals.at[neighbour_index.reshape(-1)]  48.5 us
    gather x4, local copies, waits for them, and re-layouts, edge_inputs(): gathered = jnp.take(message_rows, neighbour_block, axis=0)  34.2 us
    reduce_sum x1, other arithmetic, per_block(): return (totals, jnp.sum(grad_before, axis=1))  9.11 us
  transfers between devices with their start and end apart: 8, of which 5 were waited for; matrix products, arithmetic and copies ran while one was open for 4% of the time, Pallas kernels for 0%

commit v1 on v0

v1 whole, which is shorter than its diff:
```python
import functools
import math

import jax
import jax.numpy as jnp
from jax import lax
from jax.experimental import pallas as pl
from jax.experimental.pallas import tpu as pltpu
from jax.sharding import PartitionSpec as P

HEAD_DIM = 32
SNAPS = 8
HALO = 128
LOW = 4
F32 = jnp.float32
BF16 = jnp.bfloat16


def dot(a, b):
    return jnp.dot(a, b, preferred_element_type=F32)


def dot_t(a, b):
    return lax.dot_general(a, b, (((1,), (1,)), ((), ())), preferred_element_type=F32)


def t_dot(a, b):
    return lax.dot_general(a, b, (((0,), (0,)), ((), ())), preferred_element_type=F32)


def remote(src, dst, send, recv, device):
    return pltpu.make_async_remote_copy(
        src_ref=src,
        dst_ref=dst,
        send_sem=send,
        recv_sem=recv,
        device_id=device,
        device_id_type=pl.DeviceIdType.MESH,
    )


class Reduce:
    def __init__(self, dims, base, rows, part, fin, first, second, sems):
        self.doms, self.snaps, self.me_d, self.me_s = dims
        self.low = LOW if self.doms % LOW == 0 else 1
        self.high = self.doms // self.low
        self.group = self.low * self.snaps
        self.piece = rows // self.group
        self.base = base
        self.part, self.fin, self.first, self.second = part, fin, first, second
        self.sems = sems
        self.hi = self.me_d // self.low
        self.mine = self.me_s * self.low + self.me_d % self.low
        self.sent = []

    def member(self, t):
        return (self.hi * self.low + t % self.low, t // self.low)

    def rows_of(self, t):
        return pl.ds(pl.multiple_of(self.base + t * self.piece, 16), self.piece)

    def start(self):
        s1, r1 = self.sems[0], self.sems[1]
        for d in range(1, self.group):
            t = (self.mine + d) % self.group
            copy = remote(
                self.part.at[self.rows_of(t)],
                self.first.at[d - 1],
                s1.at[d - 1],
                r1.at[d - 1],
                self.member(t),
            )
            copy.start()
            self.sent.append(copy)
        self.one = list(self.sent)

    def middle(self):
        s2, r2 = self.sems[2], self.sems[3]
        total = self.part[self.rows_of(self.mine), :].astype(F32)
        for d in range(1, self.group):
            self.one[d - 1].wait_recv()
            total = total + self.first[d - 1].astype(F32)
        self.second[self.hi] = total.astype(BF16)
        for d in range(1, self.high):
            a = (self.hi + d) % self.high
            copy = remote(
                self.second.at[self.hi],
                self.second.at[self.hi],
                s2.at[d - 1],
                r2.at[d - 1],
                (a * self.low + self.me_d % self.low, self.me_s),
            )
            copy.start()
            self.sent.append(copy)

    def spread(self):
        s2, r2, s3, r3 = self.sems[2:]
        for d in range(1, self.high):
            a = (self.hi + self.high - d) % self.high
            remote(
                self.second.at[a],
                self.second.at[a],
                s2.at[d - 1],
                r2.at[d - 1],
                (a * self.low + self.me_d % self.low, self.me_s),
            ).wait_recv()
        total = self.second[0].astype(F32)
        for a in range(1, self.high):
            total = total + self.second[a].astype(F32)
        self.fin[self.rows_of(self.mine), :] = total.astype(BF16)
        for d in range(1, self.group):
            t = (self.mine + d) % self.group
            copy = remote(
                self.fin.at[self.rows_of(self.mine)],
                self.fin.at[self.rows_of(self.mine)],
                s3.at[d - 1],
                r3.at[d - 1],
                self.member(t),
            )
            copy.start()
            self.sent.append(copy)

    def finish(self):
        s3, r3 = self.sems[4:]
        for d in range(1, self.group):
            t = (self.mine + self.group - d) % self.group
            remote(
                self.fin.at[self.rows_of(t)],
                self.fin.at[self.rows_of(t)],
                s3.at[d - 1],
                r3.at[d - 1],
                self.member(t),
            ).wait_recv()
        for copy in self.sent:
            copy.wait_send()


def kernel(
    doms, snaps,
    feat, cot, nb, nbt, deg, wm, wc, wa, wo,
    gfeat, wout,
    ext, cat, oh, oht, wb, bef, slope, comb, spat, spsw, cosw,
    q, k, v, ga, gq, gk, gv, att, sc, gs, gsw, gsp, gb, grow, ownf, selff, ghl, ghr,
    part, first_a, second_a, first_b, second_b, fin,
    halo_s, halo_r, gho_s, gho_r, cot_s, cot_r, spa_s, spa_r, gra_s, gra_r, *red,
):
    local, nodes, width = feat.shape
    degree = nb.shape[1]
    reach = nodes + 2 * HALO
    share = nodes // snaps
    me_d, me_s = lax.axis_index("dom"), lax.axis_index("snap")
    dims = (doms, snaps, me_d, me_s)
    left, right = (me_d + doms - 1) % doms, (me_d + 1) % doms
    red_a = Reduce(dims, 0, 4 * width, part, fin, first_a, second_a, red[:6])
    red_b = Reduce(dims, 4 * width, 2 * width, part, fin, first_b, second_b, red[6:])

    barrier = pltpu.get_barrier_semaphore()

    def greet(device):
        pl.semaphore_signal(
            barrier, inc=1, device_id=device, device_id_type=pl.DeviceIdType.MESH
        )

    greet((left, me_s))
    greet((right, me_s))
    for d in range(1, red_a.group):
        greet(red_a.member((red_a.mine + d) % red_a.group))
    for d in range(1, red_a.high):
        a = (red_a.hi + d) % red_a.high
        greet((a * red_a.low + me_d % red_a.low, me_s))
    pl.semaphore_wait(barrier, red_a.group + red_a.high)

    def to_right(s):
        return remote(feat.at[s], ext.at[s, pl.ds(0, HALO)], halo_s.at[0, s], halo_r.at[0, s], (right, me_s))

    def to_left(s):
        return remote(
            feat.at[s], ext.at[s, pl.ds(reach - HALO, HALO)], halo_s.at[1, s], halo_r.at[1, s], (left, me_s)
        )

    has_left, has_right = me_d > 0, me_d < doms - 1
    for s in range(local):
        pl.when(has_right)(lambda s=s: to_right(s).start())
        pl.when(has_left)(lambda s=s: to_left(s).start())

    def my_slots():
        return pl.ds(me_s * local, local)

    def share_of(p):
        return pl.ds(pl.multiple_of(p * share, share), share)

    cot_out = []
    for d in range(1, snaps):
        p = (me_s + d) % snaps
        copy = remote(
            cot.at[:, share_of(p)], cosw.at[my_slots()], cot_s.at[d - 1], cot_r.at[d - 1], (me_d, p)
        )
        copy.start()
        cot_out.append(copy)
    for s in range(local):
        cosw[me_s * local + s] = cot[s, share_of(me_s), :]

    @pl.when(jnp.logical_not(has_left))
    def _():
        ext[:, pl.ds(0, HALO), :] = jnp.zeros((local, HALO, width), BF16)
        ghl[...] = jnp.zeros(ghl.shape, BF16)

    @pl.when(jnp.logical_not(has_right))
    def _():
        ext[:, pl.ds(reach - HALO, HALO), :] = jnp.zeros((local, HALO, width), BF16)
        ghr[...] = jnp.zeros(ghr.shape, BF16)

    ext[:, pl.ds(HALO, nodes), :] = feat[...]

    first_row = me_d * nodes - HALO
    index = nb[...] - first_row
    index_t = nbt[...] - first_row
    lanes = lax.broadcasted_iota(jnp.int32, (nodes, reach), 1)
    subs = lax.broadcasted_iota(jnp.int32, (reach, nodes), 0)
    eye = jnp.where(
        lax.broadcasted_iota(jnp.int32, (nodes, nodes), 0)
        == lax.broadcasted_iota(jnp.int32, (nodes, nodes), 1),
        1.0,
        0.0,
    ).astype(BF16)
    counts = deg[...]
    inverse = 1.0 / counts.astype(F32)
    for j in range(degree):
        at = pl.ds(j * nodes, nodes)
        oh[at, pl.ds(0, reach)] = jnp.where(lanes == index[:, j : j + 1], 1.0, 0.0).astype(BF16)
        oh[at, pl.ds(reach, nodes)] = eye
        oht[pl.ds(0, reach), at] = jnp.where(subs == index_t[j : j + 1, :], 1.0, 0.0).astype(BF16)
        oht[pl.ds(reach, nodes), at] = eye
        wb[at, :] = jnp.broadcast_to(jnp.where(counts > j, inverse, 0.0), (nodes, 128))

    block = 32
    spa_out = []
    for s in range(local):
        pl.when(has_left)(lambda s=s: to_right(s).wait_recv())
        pl.when(has_right)(lambda s=s: to_left(s).wait_recv())
        cat[pl.ds(0, reach), :] = dot(ext[s], wm[...]).astype(BF16)
        cat[pl.ds(reach, nodes), :] = feat[s]
        bef[...] = dot(oh[...], cat[...])

        def forward(c, carry, s=s):
            total = jnp.zeros((block, width), F32)
            for j in range(degree):
                at = pl.ds(pl.multiple_of(j * nodes + c * block, block), block)
                x = bef[at, :]
                w = wb[at, :]
                w = jnp.concatenate([w] * (width // 128), axis=1)
                g = 0.5 * jnp.tanh(0.5 * x) + 0.5
                y = x * g
                total = total + w * y
                slope[s, at, :] = (w * (g + y * (1.0 - g))).astype(BF16)
            comb[s, pl.ds(pl.multiple_of(c * block, block), block), :] = total.astype(BF16)
            return carry

        lax.fori_loop(0, nodes // block, forward, 0)
        spat[s] = (feat[s].astype(F32) + dot(comb[s], wc[...])).astype(BF16)
        for d in range(1, snaps):
            p = (me_s + d) % snaps
            copy = remote(
                spat.at[s, share_of(p)],
                spsw.at[me_s * local + s],
                spa_s.at[s, d - 1],
                spa_r.at[s, d - 1],
                (me_d, p),
            )
            copy.start()
            spa_out.append((s, d, copy))
        spsw[me_s * local + s] = spat[s, share_of(me_s), :]

    rows = SNAPS * share
    for copy in cot_out:
        copy.wait_recv()
    flat_cot = cosw[...].reshape(rows, width)
    ga[...] = dot_t(flat_cot, wo[...])
    for s, d, copy in spa_out:
        copy.wait_recv()
    flat_spat = spsw[...].reshape(rows, width)
    q[...] = dot(flat_spat, wa[:, 0:width])
    k[...] = dot(flat_spat, wa[:, width : 2 * width])
    v[...] = dot(flat_spat, wa[:, 2 * width : 3 * width])
    root = 1.0 / math.sqrt(HEAD_DIM)
    heads = jnp.where(
        lax.broadcasted_iota(jnp.int32, (width, width), 0) // HEAD_DIM
        == lax.broadcasted_iota(jnp.int32, (width, width), 1) // HEAD_DIM,
        1.0,
        0.0,
    ).astype(BF16)

    def pairs(s, carry):
        at = pl.ds(pl.multiple_of(s * share, share), share)
        out = pl.ds(pl.multiple_of(s * rows, rows), rows)
        mine = q[at, :] * root
        other = ga[at, :]
        sc[out, :] = dot(
            (k[...].reshape(SNAPS, share, width) * mine[None]).astype(BF16).reshape(rows, width), heads
        )
        gs[out, :] = dot(
            (v[...].reshape(SNAPS, share, width) * other[None]).astype(BF16).reshape(rows, width), heads
        )
        return carry

    lax.fori_loop(0, SNAPS, pairs, 0)

    small = 8

    def attend(c, carry):
        def at(s):
            return pl.ds(pl.multiple_of(s * share + c * small, small), small)

        gk_sum = [jnp.zeros((small, width), F32)] * SNAPS
        gv_sum = [jnp.zeros((small, width), F32)] * SNAPS
        for s in range(SNAPS):
            e = [jnp.exp(sc[at(s * SNAPS + r), :]) for r in range(SNAPS)]
            norm = 1.0 / sum(e[1:], e[0])
            w = [x * norm for x in e]
            g = [gs[at(s * SNAPS + r), :] for r in range(SNAPS)]
            prods = [x * y for x, y in zip(w, g)]
            mean = sum(prods[1:], prods[0])
            mine, other = q[at(s), :], ga[at(s), :]
            att_sum = jnp.zeros((small, width), F32)
            gq_sum = jnp.zeros((small, width), F32)
            for r in range(SNAPS):
                t = w[r] * (g[r] - mean)
                att_sum = att_sum + w[r] * v[at(r), :]
                gq_sum = gq_sum + t * k[at(r), :]
                gk_sum[r] = gk_sum[r] + t * mine
                gv_sum[r] = gv_sum[r] + w[r] * other
            att[at(s), :] = att_sum
            gq[at(s), :] = gq_sum * root
        for r in range(SNAPS):
            gk[at(r), :] = gk_sum[r] * root
            gv[at(r), :] = gv_sum[r]
        return carry

    lax.fori_loop(0, share // small, attend, 0)

    g3 = [gq[...].astype(BF16), gk[...].astype(BF16), gv[...].astype(BF16)]
    back = flat_cot.astype(F32)
    for n in range(3):
        back = back + dot_t(g3[n], wa[:, n * width : (n + 1) * width])
    gsw[...] = back.astype(BF16).reshape(SNAPS, share, width)
    gra_out = []
    for d in range(1, snaps):
        p = (me_s + d) % snaps
        copy = remote(
            gsw.at[pl.ds(p * local, local)],
            gsp.at[:, share_of(me_s)],
            gra_s.at[d - 1],
            gra_r.at[d - 1],
            (me_d, p),
        )
        copy.start()
        gra_out.append(copy)
    for s in range(local):
        gsp[s, share_of(me_s), :] = gsw[me_s * local + s]
    part[pl.ds(0, width), :] = t_dot(att[...].astype(BF16), flat_cot).astype(BF16)
    for n in range(3):
        part[pl.ds((n + 1) * width, width), :] = t_dot(flat_spat, g3[n]).astype(BF16)
    red_a.start()
    for d in range(1, snaps):
        p = (me_s + snaps - d) % snaps
        remote(
            gsw.at[pl.ds(p * local, local)],
            gsp.at[:, share_of(p)],
            gra_s.at[d - 1],
            gra_r.at[d - 1],
            (me_d, p),
        ).wait_recv()

    def ghost_left(s):
        return remote(grow.at[s, pl.ds(0, HALO)], ghr.at[s], gho_s.at[0, s], gho_r.at[0, s], (left, me_s))

    def ghost_right(s):
        return remote(
            grow.at[s, pl.ds(reach - HALO, HALO)], ghl.at[s], gho_s.at[1, s], gho_r.at[1, s], (right, me_s)
        )

    part[pl.ds(4 * width, width), :] = t_dot(
        comb[...].reshape(local * nodes, width), gsp[...].reshape(local * nodes, width)
    ).astype(BF16)
    for s in range(local):
        bef[pl.ds(0, nodes), :] = dot_t(gsp[s], wc[...])

        def backward(c, carry, s=s):
            gc = bef[pl.ds(pl.multiple_of(c * block, block), block), :]
            for j in range(degree):
                at = pl.ds(pl.multiple_of(j * nodes + c * block, block), block)
                gb[at, :] = (gc * slope[s, at, :].astype(F32)).astype(BF16)
            return carry

        lax.fori_loop(0, nodes // block, backward, 0)
        sums = dot(oht[...], gb[...])
        grow[s] = sums[:reach].astype(BF16)
        ownf[s] = sums[HALO : HALO + nodes]
        selff[s] = sums[reach:]
        pl.when(has_left)(lambda s=s: ghost_left(s).start())
        pl.when(has_right)(lambda s=s: ghost_right(s).start())
        if s == local // 2:
            red_a.middle()
    part[pl.ds(5 * width, width), :] = t_dot(
        ext[...].reshape(local * reach, width), grow[...].reshape(local * reach, width)
    ).astype(BF16)
    red_b.start()
    red_a.spread()
    for s in range(local):
        pl.when(has_right)(lambda s=s: ghost_left(s).wait_recv())
        pl.when(has_left)(lambda s=s: ghost_right(s).wait_recv())
        if s == local // 2:
            red_b.middle()
        own = ownf[s] + ghl[s].astype(F32) + ghr[s].astype(F32)
        here = gsp[s].astype(F32) + selff[s] + dot_t(own.astype(BF16), wm[...])
        gfeat[s] = here.astype(BF16)
    red_b.spread()
    red_a.finish()
    red_b.finish()
    wout[...] = fin[...]
    for s in range(local):
        @pl.when(has_right)
        def _(s=s):
            to_right(s).wait_send()
            ghost_right(s).wait_send()

        @pl.when(has_left)
        def _(s=s):
            to_left(s).wait_send()
            ghost_left(s).wait_send()
    for copy in cot_out + [c for _, _, c in spa_out] + gra_out:
        copy.wait_send()


def body(doms, snaps, features, cotangent, neighbours, degrees, message_proj, combine_proj, attend_proj, output_proj):
    local, nodes, width = features.shape
    degree = neighbours.shape[1]
    reach = nodes + 2 * HALO
    share = nodes // snaps
    rows = SNAPS * share
    low = LOW if doms % LOW == 0 else 1
    high, group = doms // low, low * snaps
    dma = pltpu.SemaphoreType.DMA
    vmem = pltpu.VMEM

    def reduce_sems():
        g, h = (max(group - 1, 1),), (max(high - 1, 1),)
        return [dma(g), dma(g), dma(h), dma(h), dma(g), dma(g)]

    peers = max(snaps - 1, 1)
    gfeat, wout = pl.pallas_call(
        functools.partial(kernel, doms, snaps),
        out_shape=(
            jax.ShapeDtypeStruct(features.shape, BF16),
            jax.ShapeDtypeStruct((6 * width, width), BF16),
        ),
        in_specs=[pl.BlockSpec(memory_space=pltpu.VMEM)] * 9,
        out_specs=[pl.BlockSpec(memory_space=pltpu.VMEM)] * 2,
        scratch_shapes=[
            vmem((local, reach, width), BF16),
            vmem((reach + nodes, width), BF16),
            vmem((degree * nodes, reach + nodes), BF16),
            vmem((reach + nodes, degree * nodes), BF16),
            vmem((degree * nodes, 128), F32),
            vmem((degree * nodes, width), F32),
            vmem((local, degree * nodes, width), BF16),
            vmem((local, nodes, width), BF16),
            vmem((local, nodes, width), BF16),
            vmem((SNAPS, share, width), BF16),
            vmem((SNAPS, share, width), BF16),
            *[vmem((rows, width), F32)] * 8,
            vmem((SNAPS * rows, width), F32),
            vmem((SNAPS * rows, width), F32),
            vmem((SNAPS, share, width), BF16),
            vmem((local, nodes, width), BF16),
            vmem((degree * nodes, width), BF16),
            vmem((local, reach, width), BF16),
            vmem((local, nodes, width), F32),
            vmem((local, nodes, width), F32),
            vmem((local, HALO, width), BF16),
            vmem((local, HALO, width), BF16),
            vmem((6 * width, width), BF16),
            vmem((group - 1, 4 * width // group, width), BF16),
            vmem((high, 4 * width // group, width), BF16),
            vmem((group - 1, 2 * width // group, width), BF16),
            vmem((high, 2 * width // group, width), BF16),
            vmem((6 * width, width), BF16),
            dma((2, local)),
            dma((2, local)),
            dma((2, local)),
            dma((2, local)),
            dma((peers,)),
            dma((peers,)),
            dma((local, peers)),
            dma((local, peers)),
            dma((peers,)),
            dma((peers,)),
            *reduce_sems(),
            *reduce_sems(),
        ],
        compiler_params=pltpu.CompilerParams(
            collective_id=0, has_side_effects=True, vmem_limit_bytes=56 * 2**20
        ),
    )(
        features, cotangent, neighbours, neighbours.T, degrees.reshape(nodes, 1),
        message_proj, combine_proj, attend_proj, output_proj,
    )
    factor = 1.0 / math.sqrt(SNAPS * doms * nodes)
    block = [wout[n * width : (n + 1) * width].astype(F32) * factor for n in range(6)]
    return (gfeat, block[5], block[4], jnp.concatenate(block[1:4], axis=1), block[0])


def solution(mesh):
    in_specs = (
        P("snap", "dom", None),
        P("snap", "dom", None),
        P("dom", None),
        P("dom"),
        P(),
        P(),
        P(),
        P(),
    )
    out_specs = (P("snap", "dom", None), P(), P(), P(), P())
    return jax.shard_map(
        functools.partial(body, mesh.shape["dom"], mesh.shape["snap"]),
        mesh=mesh,
        in_specs=in_specs,
        out_specs=out_specs,
        check_vma=False,
    )
```

time: 383 us -> 66.7 us (0.17)
  the two profiles are of different devices: /device:TPU:0 before, /device:TPU:11 now
where the time goes in v1:
time: 66.7 us; the launch traced here: 66.4 us
  Pallas kernels  59.9 us (90%)
  other arithmetic  3.06 us (5%)
  local copies, waits for them, and re-layouts  2.87 us (4%)
    pallas_call x1, Pallas kernels, body(): pl.pallas_call(functools.partial(kernel, doms, snaps), out_shape=(jax.Sha...  59.9 us
    mul x1, other arithmetic, body(): wout[n * width:(n + 1) * width].astype(F32) * factor  2.13 us
    unnamed x8, local copies, waits for them, and re-layouts  2.13 us

profile of v1, /device:TPU:11, one launch (start us, length us, event | category | flops | bytes accessed | tf_op | source)
XLA Modules:
  0.0 66.4 jit_solution(7588189102003752372)
XLA Ops:
  0.6 0.0 copy-start.2
  0.6 0.6 copy-done.2
  1.3 0.0 copy-start.1
  1.3 0.7 %copy.14.deg = s32[128,1]{1,0:T(8,128)} copy(s32[128,1]{0,1:T(1,128)S(1)} %bitcast.3) | data formatting | bytes 1024 | tf_op jit(solution)/shard_map/reshape | solution.py:505
  2.0 0.0 copy-done.1
  2.0 0.7 %copy.13.nb = s32[128,16]{1,0:T(8,128)} copy(s32[128,16]{0,1:T(8,128)S(1)} %copy-done.1) | data formatting | bytes 16384 | tf_op args[2]
  2.8 59.9 %shard_map.119 = (bf16[4,128,256]{2,1,0:T(8,128)(2,1)}, bf16[1536,256]{1,0:T(8,128)(2,1)}) custom-call(bf16[4,128,256]{2,1,0:T(8,128)(2,1)} %feat.1, bf16[4,128,256]{2,1,0:T(8,128)(2,1)} %cot.1, s32[128,16]{1,0:T(8,128)} %copy.13.nb, s32[16,128]{1,0:T(8,128)} %bitcast.2, s32[128,1]{1,0:T(8,128)} %copy.14.deg, bf16[256,256]{1,0:T(8,128)(2,1)} %wm.1, ...), custom_call_target="tpu_custom_call" | custom-call | tf_op jit(solution)/shard_map/pallas_call | solution.py:451
  62.6 2.1 %convert_multiply_fusion = (f32[256,256]{1,0:T(8,128)}, f32[256,256]{1,0:T(8,128)S(1)}, f32[256,256]{1,0:T(8,128)S(1)}, f32[256,256]{1,0:T(8,128)S(1)}, f32[256,256]{1,0:T(8,128)}, /*index=5*/f32[256,256]{1,0:T(8,128)}) fusion(bf16[1536,256]{1,0:T(8,128)(2,1)} %get-tuple-element.8), kind=kLoop, calls=%fused_computation.1 | loop fusion | flops 786432 | bytes 2359296 | tf_op jit(solution)/shard_map/mul | solution.py:509
  64.8 0.0 copy-start
  64.8 0.9 %pad_maximum_fusion = f32[256,768]{1,0:T(8,128)} fusion(f32[256,256]{1,0:T(8,128)S(1)} %get-tuple-element.10, f32[256,256]{1,0:T(8,128)S(1)} %get-tuple-element.11, f32[256,256]{1,0:T(8,128)S(1)} %get-tuple-element.12), kind=kLoop, calls=%fused_computation | loop fusion | flops 393216 | bytes 1572864 | tf_op jit(solution)/shard_map/concatenate | solution.py:510
  65.7 0.0 copy-done
  65.7 0.7 %copy.16 = bf16[4,128,256]{2,1,0:T(8,128)(2,1)} copy(bf16[4,128,256]{2,1,0:T(8,128)(2,1)S(1)} %copy-done) | data formatting | bytes 524288
Async XLA Ops:
  0.6 0.7 copy-start.2
  1.3 0.7 %copy-start.1 = (s32[128,16]{0,1:T(8,128)S(1)}, s32[128,16]{0,1:T(8,128)}, u32[]{:S(2)}) copy-start(s32[128,16]{0,1:T(8,128)} %param.10) | copy-start | bytes 24580
  64.8 1.0 %copy-start = (bf16[4,128,256]{2,1,0:T(8,128)(2,1)S(1)}, bf16[4,128,256]{2,1,0:T(8,128)(2,1)}, u32[]{:S(2)}) copy-start(bf16[4,128,256]{2,1,0:T(8,128)(2,1)} %get-tuple-element.20) | copy-start | bytes 786436

commit v2 on v1

--- a/solution.py
+++ b/solution.py
@@ -137,11 +137,11 @@
 
 def kernel(
     doms, snaps,
-    feat, cot, nb, nbt, deg, wm, wc, wa, wo,
+    feat, cot, nb, deg, wm, wc, wa, wo,
     gfeat, wout,
-    ext, cat, oh, oht, wb, bef, slope, comb, spat, spsw, cosw,
-    q, k, v, ga, gq, gk, gv, att, sc, gs, gsw, gsp, gb, grow, ownf, selff, ghl, ghr,
-    part, first_a, second_a, first_b, second_b, fin,
+    ext, cat, oh, oht, wb, slope, comb, spat, spsw, cosw,
+    q, k, v, ga, gq, gk, gv, att, gsw, gsp, grow, ownf, selff, ghl, ghr,
+    part, first_a, second_a, first_b, second_b, first_c, second_c, fin,
     halo_s, halo_r, gho_s, gho_r, cot_s, cot_r, spa_s, spa_r, gra_s, gra_r, *red,
 ):
     local, nodes, width = feat.shape
@@ -151,8 +151,15 @@
     me_d, me_s = lax.axis_index("dom"), lax.axis_index("snap")
     dims = (doms, snaps, me_d, me_s)
     left, right = (me_d + doms - 1) % doms, (me_d + 1) % doms
-    red_a = Reduce(dims, 0, 4 * width, part, fin, first_a, second_a, red[:6])
-    red_b = Reduce(dims, 4 * width, 2 * width, part, fin, first_b, second_b, red[6:])
+    halves = width // 128
+    unit = halves * width
+    red_a = Reduce(dims, 0, 4 * unit, part, fin, first_a, second_a, red[:6])
+    red_b = Reduce(dims, 4 * unit, unit, part, fin, first_b, second_b, red[6:12])
+    red_c = Reduce(dims, 5 * unit, unit, part, fin, first_c, second_c, red[12:])
+
+    def put(n, value):
+        for h in range(halves):
+            part[pl.ds(n * unit + h * width, width), :] = value[:, h * 128 : (h + 1) * 128].astype(BF16)
 
     barrier = pltpu.get_barrier_semaphore()
 
@@ -214,7 +221,7 @@
 
     first_row = me_d * nodes - HALO
     index = nb[...] - first_row
-    index_t = nbt[...] - first_row
+    index_t = jnp.concatenate([index] * (nodes // degree), axis=1).T
     lanes = lax.broadcasted_iota(jnp.int32, (nodes, reach), 1)
     subs = lax.broadcasted_iota(jnp.int32, (reach, nodes), 0)
     eye = jnp.where(
@@ -223,40 +230,38 @@
         1.0,
         0.0,
     ).astype(BF16)
-    counts = deg[...]
+    counts = jnp.broadcast_to(deg[...], (nodes, nodes)).T
     inverse = 1.0 / counts.astype(F32)
+    block = nodes // 2
     for j in range(degree):
         at = pl.ds(j * nodes, nodes)
-        oh[at, pl.ds(0, reach)] = jnp.where(lanes == index[:, j : j + 1], 1.0, 0.0).astype(BF16)
-        oh[at, pl.ds(reach, nodes)] = eye
+        hit = jnp.where(lanes == index[:, j : j + 1], 1.0, 0.0).astype(BF16)
+        for c in range(nodes // block):
+            to = pl.ds((c * degree + j) * block, block)
+            oh[to, pl.ds(0, reach)] = hit[c * block : (c + 1) * block]
+            oh[to, pl.ds(reach, nodes)] = eye[c * block : (c + 1) * block]
         oht[pl.ds(0, reach), at] = jnp.where(subs == index_t[j : j + 1, :], 1.0, 0.0).astype(BF16)
         oht[pl.ds(reach, nodes), at] = eye
-        wb[at, :] = jnp.broadcast_to(jnp.where(counts > j, inverse, 0.0), (nodes, 128))
-
-    block = 32
+        wb[at, :] = jnp.where(counts > j, inverse, 0.0)
+
     spa_out = []
     for s in range(local):
         pl.when(has_left)(lambda s=s: to_right(s).wait_recv())
         pl.when(has_right)(lambda s=s: to_left(s).wait_recv())
         cat[pl.ds(0, reach), :] = dot(ext[s], wm[...]).astype(BF16)
         cat[pl.ds(reach, nodes), :] = feat[s]
-        bef[...] = dot(oh[...], cat[...])
-
-        def forward(c, carry, s=s):
+        for c in range(nodes // block):
+            before = dot(oh[pl.ds(c * degree * block, degree * block), :], cat[...])
             total = jnp.zeros((block, width), F32)
             for j in range(degree):
-                at = pl.ds(pl.multiple_of(j * nodes + c * block, block), block)
-                x = bef[at, :]
-                w = wb[at, :]
-                w = jnp.concatenate([w] * (width // 128), axis=1)
+                at = pl.ds(j * nodes + c * block, block)
+                x = before[j * block : (j + 1) * block]
+                w = jnp.concatenate([wb[at, :]] * halves, axis=1)
                 g = 0.5 * jnp.tanh(0.5 * x) + 0.5
                 y = x * g
                 total = total + w * y
                 slope[s, at, :] = (w * (g + y * (1.0 - g))).astype(BF16)
-            comb[s, pl.ds(pl.multiple_of(c * block, block), block), :] = total.astype(BF16)
-            return carry
-
-        lax.fori_loop(0, nodes // block, forward, 0)
+            comb[s, pl.ds(c * block, block), :] = total.astype(BF16)
         spat[s] = (feat[s].astype(F32) + dot(comb[s], wc[...])).astype(BF16)
         for d in range(1, snaps):
             p = (me_s + d) % snaps
@@ -290,43 +295,44 @@
         0.0,
     ).astype(BF16)
 
-    def pairs(s, carry):
-        at = pl.ds(pl.multiple_of(s * share, share), share)
-        out = pl.ds(pl.multiple_of(s * rows, rows), rows)
-        mine = q[at, :] * root
-        other = ga[at, :]
-        sc[out, :] = dot(
-            (k[...].reshape(SNAPS, share, width) * mine[None]).astype(BF16).reshape(rows, width), heads
-        )
-        gs[out, :] = dot(
-            (v[...].reshape(SNAPS, share, width) * other[None]).astype(BF16).reshape(rows, width), heads
-        )
-        return carry
-
-    lax.fori_loop(0, SNAPS, pairs, 0)
-
-    small = 8
+    small = 16
 
     def attend(c, carry):
         def at(s):
             return pl.ds(pl.multiple_of(s * share + c * small, small), small)
 
+        def piece(values, s, r):
+            n = (s * SNAPS + r) * small
+            return values[n : n + small]
+
+        mines = [q[at(s), :] for s in range(SNAPS)]
+        others = [ga[at(s), :] for s in range(SNAPS)]
+        ks = [k[at(r), :] for r in range(SNAPS)]
+        vs = [v[at(r), :] for r in range(SNAPS)]
+        sc = dot(
+            jnp.concatenate([(mines[s] * root * ks[r]).astype(BF16) for s in range(SNAPS) for r in range(SNAPS)]),
+            heads,
+        )
+        gs = dot(
+            jnp.concatenate([(others[s] * vs[r]).astype(BF16) for s in range(SNAPS) for r in range(SNAPS)]),
+            heads,
+        )
         gk_sum = [jnp.zeros((small, width), F32)] * SNAPS
         gv_sum = [jnp.zeros((small, width), F32)] * SNAPS
         for s in range(SNAPS):
-            e = [jnp.exp(sc[at(s * SNAPS + r), :]) for r in range(SNAPS)]
+            e = [jnp.exp(piece(sc, s, r)) for r in range(SNAPS)]
             norm = 1.0 / sum(e[1:], e[0])
             w = [x * norm for x in e]
-            g = [gs[at(s * SNAPS + r), :] for r in range(SNAPS)]
+            g = [piece(gs, s, r) for r in range(SNAPS)]
             prods = [x * y for x, y in zip(w, g)]
             mean = sum(prods[1:], prods[0])
-            mine, other = q[at(s), :], ga[at(s), :]
+            mine, other = mines[s], others[s]
             att_sum = jnp.zeros((small, width), F32)
             gq_sum = jnp.zeros((small, width), F32)
             for r in range(SNAPS):
                 t = w[r] * (g[r] - mean)
-                att_sum = att_sum + w[r] * v[at(r), :]
-                gq_sum = gq_sum + t * k[at(r), :]
+                att_sum = att_sum + w[r] * vs[r]
+                gq_sum = gq_sum + t * ks[r]
                 gk_sum[r] = gk_sum[r] + t * mine
                 gv_sum[r] = gv_sum[r] + w[r] * other
             att[at(s), :] = att_sum
@@ -357,9 +363,9 @@
         gra_out.append(copy)
     for s in range(local):
         gsp[s, share_of(me_s), :] = gsw[me_s * local + s]
-    part[pl.ds(0, width), :] = t_dot(att[...].astype(BF16), flat_cot).astype(BF16)
+    put(0, t_dot(att[...].astype(BF16), flat_cot))
     for n in range(3):
-        part[pl.ds((n + 1) * width, width), :] = t_dot(flat_spat, g3[n]).astype(BF16)
+        put(n + 1, t_dot(flat_spat, g3[n]))
     red_a.start()
     for d in range(1, snaps):
         p = (me_s + snaps - d) % snaps
@@ -379,21 +385,16 @@
             grow.at[s, pl.ds(reach - HALO, HALO)], ghl.at[s], gho_s.at[1, s], gho_r.at[1, s], (right, me_s)
         )
 
-    part[pl.ds(4 * width, width), :] = t_dot(
-        comb[...].reshape(local * nodes, width), gsp[...].reshape(local * nodes, width)
-    ).astype(BF16)
-    for s in range(local):
-        bef[pl.ds(0, nodes), :] = dot_t(gsp[s], wc[...])
-
-        def backward(c, carry, s=s):
-            gc = bef[pl.ds(pl.multiple_of(c * block, block), block), :]
-            for j in range(degree):
-                at = pl.ds(pl.multiple_of(j * nodes + c * block, block), block)
-                gb[at, :] = (gc * slope[s, at, :].astype(F32)).astype(BF16)
-            return carry
-
-        lax.fori_loop(0, nodes // block, backward, 0)
-        sums = dot(oht[...], gb[...])
+    put(
+        4, t_dot(comb[...].reshape(local * nodes, width), gsp[...].reshape(local * nodes, width))
+    )
+    red_b.start()
+    for s in range(local):
+        gc = dot_t(gsp[s], wc[...])
+        gb = jnp.concatenate(
+            [(gc * slope[s, pl.ds(j * nodes, nodes), :].astype(F32)).astype(BF16) for j in range(degree)]
+        )
+        sums = dot(oht[...], gb)
         grow[s] = sums[:reach].astype(BF16)
         ownf[s] = sums[HALO : HALO + nodes]
         selff[s] = sums[reach:]
@@ -401,22 +402,25 @@
         pl.when(has_right)(lambda s=s: ghost_right(s).start())
         if s == local // 2:
             red_a.middle()
-    part[pl.ds(5 * width, width), :] = t_dot(
-        ext[...].reshape(local * reach, width), grow[...].reshape(local * reach, width)
-    ).astype(BF16)
-    red_b.start()
+    put(
+        5, t_dot(ext[...].reshape(local * reach, width), grow[...].reshape(local * reach, width))
+    )
+    red_c.start()
+    red_b.middle()
     red_a.spread()
     for s in range(local):
         pl.when(has_right)(lambda s=s: ghost_left(s).wait_recv())
         pl.when(has_left)(lambda s=s: ghost_right(s).wait_recv())
         if s == local // 2:
-            red_b.middle()
+            red_c.middle()
         own = ownf[s] + ghl[s].astype(F32) + ghr[s].astype(F32)
         here = gsp[s].astype(F32) + selff[s] + dot_t(own.astype(BF16), wm[...])
         gfeat[s] = here.astype(BF16)
     red_b.spread()
+    red_c.spread()
     red_a.finish()
     red_b.finish()
+    red_c.finish()
     wout[...] = fin[...]
     for s in range(local):
         @pl.when(has_right)
@@ -432,12 +436,24 @@
         copy.wait_send()
 
 
+def finish(factor, gfeat, wout, features, message, combine, attend, output):
+    features[...] = gfeat[...]
+    width = message.shape[0]
+    homes = ((output, 0), (attend, 0), (attend, width), (attend, 2 * width), (combine, 0), (message, 0))
+    row = 0
+    for ref, column in homes:
+        for h in range(width // 128):
+            ref[:, pl.ds(column + h * 128, 128)] = wout[pl.ds(row, width), :].astype(F32) * factor
+            row += width
+
+
 def body(doms, snaps, features, cotangent, neighbours, degrees, message_proj, combine_proj, attend_proj, output_proj):
     local, nodes, width = features.shape
     degree = neighbours.shape[1]
     reach = nodes + 2 * HALO
     share = nodes // snaps
     rows = SNAPS * share
+    unit = width // 128 * width
     low = LOW if doms % LOW == 0 else 1
     high, group = doms // low, low * snaps
     dma = pltpu.SemaphoreType.DMA
@@ -452,9 +468,9 @@
         functools.partial(kernel, doms, snaps),
         out_shape=(
             jax.ShapeDtypeStruct(features.shape, BF16),
-            jax.ShapeDtypeStruct((6 * width, width), BF16),
+            jax.ShapeDtypeStruct((6 * unit, 128), BF16),
         ),
-        in_specs=[pl.BlockSpec(memory_space=pltpu.VMEM)] * 9,
+        in_specs=[pl.BlockSpec(memory_space=pltpu.VMEM)] * 8,
         out_specs=[pl.BlockSpec(memory_space=pltpu.VMEM)] * 2,
         scratch_shapes=[
             vmem((local, reach, width), BF16),
@@ -462,29 +478,26 @@
             vmem((degree * nodes, reach + nodes), BF16),
             vmem((reach + nodes, degree * nodes), BF16),
             vmem((degree * nodes, 128), F32),
-            vmem((degree * nodes, width), F32),
             vmem((local, degree * nodes, width), BF16),
             vmem((local, nodes, width), BF16),
             vmem((local, nodes, width), BF16),
             vmem((SNAPS, share, width), BF16),
             vmem((SNAPS, share, width), BF16),
             *[vmem((rows, width), F32)] * 8,
-            vmem((SNAPS * rows, width), F32),
-            vmem((SNAPS * rows, width), F32),
             vmem((SNAPS, share, width), BF16),
             vmem((local, nodes, width), BF16),
-            vmem((degree * nodes, width), BF16),
             vmem((local, reach, width), BF16),
             vmem((local, nodes, width), F32),
             vmem((local, nodes, width), F32),
             vmem((local, HALO, width), BF16),
             vmem((local, HALO, width), BF16),
-            vmem((6 * width, width), BF16),
-            vmem((group - 1, 4 * width // group, width), BF16),
-            vmem((high, 4 * width // group, width), BF16),
-            vmem((group - 1, 2 * width // group, width), BF16),
-            vmem((high, 2 * width // group, width), BF16),
-            vmem((6 * width, width), BF16),
+            vmem((6 * unit, 128), BF16),
+            *[
+                vmem((count, size // group, 128), BF16)
+                for size in (4 * unit, unit, unit)
+                for count in (group - 1, high)
+            ],
+            vmem((6 * unit, 128), BF16),
             dma((2, local)),
             dma((2, local)),
             dma((2, local)),
@@ -497,17 +510,29 @@
             dma((peers,)),
             *reduce_sems(),
             *reduce_sems(),
+            *reduce_sems(),
         ],
         compiler_params=pltpu.CompilerParams(
             collective_id=0, has_side_effects=True, vmem_limit_bytes=56 * 2**20
         ),
     )(
-        features, cotangent, neighbours, neighbours.T, degrees.reshape(nodes, 1),
+        features, cotangent, neighbours, degrees.reshape(1, nodes),
         message_proj, combine_proj, attend_proj, output_proj,
     )
     factor = 1.0 / math.sqrt(SNAPS * doms * nodes)
-    block = [wout[n * width : (n + 1) * width].astype(F32) * factor for n in range(6)]
-    return (gfeat, block[5], block[4], jnp.concatenate(block[1:4], axis=1), block[0])
+    square = jax.ShapeDtypeStruct((width, width), F32)
+    return pl.pallas_call(
+        functools.partial(finish, factor),
+        out_shape=(
+            jax.ShapeDtypeStruct(features.shape, BF16),
+            square,
+            square,
+            jax.ShapeDtypeStruct((width, 3 * width), F32),
+            square,
+        ),
+        in_specs=[pl.BlockSpec(memory_space=pltpu.VMEM)] * 2,
+        out_specs=[pl.BlockSpec(memory_space=pltpu.VMEM)] * 5,
+    )(gfeat, wout)
 
 
 def solution(mesh):

time: 66.7 us -> 61.1 us (0.916)
  other arithmetic: 3.06 us -> 0 us
  local copies, waits for them, and re-layouts: 2.87 us -> 1.43 us
  Pallas kernels: 59.9 us -> 58.8 us
    pallas_call x1, Pallas kernels: 59.9 us -> 56.3 us  [body(): pl.pallas_call(functools.partial(kernel, doms, snaps), out_shape=(jax.Sha...]
    pallas_call x0 -> x1, Pallas kernels: none -> 2.5 us  [body(): pl.pallas_call(functools.partial(finish, factor), out_shape=(jax.ShapeDty...]
    mul x1 -> x0, other arithmetic: 2.13 us -> none  [body(): wout[n * width:(n + 1) * width].astype(F32) * factor]
    concatenate x1 -> x0, other arithmetic: 0.93 us -> none  [body(): jnp.concatenate(block[1:4], axis=1)]
    reshape x1 -> x0, local copies, waits for them, and re-layouts: 0.74 us -> none  [body(): degrees.reshape(nodes, 1)]
    unnamed x8 -> x1, local copies, waits for them, and re-layouts: 2.13 us -> 1.43 us
where the time goes in v2:
time: 61.1 us; the launch traced here: 60.9 us
  Pallas kernels  58.8 us (96%)
  local copies, waits for them, and re-layouts  1.43 us (2%)
  between operations  0.64 us (1%)
    pallas_call x1, Pallas kernels, body(): pl.pallas_call(functools.partial(kernel, doms, snaps), out_shape=(jax.Sha...  56.3 us
    pallas_call x1, Pallas kernels, body(): pl.pallas_call(functools.partial(finish, factor), out_shape=(jax.ShapeDty...  2.5 us
    unnamed x1, local copies, waits for them, and re-layouts  1.43 us

profile of v2, /device:TPU:11, one launch (start us, length us, event | category | flops | bytes accessed | tf_op | source)
XLA Modules:
  0.0 60.9 jit_solution(13855711414737642433)
XLA Ops:
  0.6 1.4 %copy.13.nb = s32[128,16]{1,0:T(8,128)} copy(s32[128,16]{0,1:T(8,128)} %param.10) | data formatting | bytes 16384 | tf_op args[2]
  2.1 56.3 %shard_map.119 = (bf16[4,128,256]{2,1,0:T(8,128)(2,1)}, bf16[3072,128]{1,0:T(8,128)(2,1)}) custom-call(bf16[4,128,256]{2,1,0:T(8,128)(2,1)} %feat.1, bf16[4,128,256]{2,1,0:T(8,128)(2,1)} %cot.1, s32[128,16]{1,0:T(8,128)} %copy.13.nb, s32[1,128]{1,0:T(1,128)} %bitcast.1, bf16[256,256]{1,0:T(8,128)(2,1)} %wm.1, bf16[256,256]{1,0:T(8,128)(2,1)} %wc.1, ...), custom_call_target="tpu_custom_call" | custom-call | tf_op jit(solution)/shard_map/pallas_call | solution.py:467
  58.4 2.5 %shard_map.120 = (bf16[4,128,256]{2,1,0:T(8,128)(2,1)}, f32[256,256]{1,0:T(8,128)}, f32[256,256]{1,0:T(8,128)}, f32[256,768]{1,0:T(8,128)}, f32[256,256]{1,0:T(8,128)}) custom-call(bf16[4,128,256]{2,1,0:T(8,128)(2,1)} %get-tuple-element.7.gfeat, bf16[3072,128]{1,0:T(8,128)(2,1)} %get-tuple-element.8.wout), custom_call_target="tpu_custom_call" | custom-call | tf_op jit(solution)/shard_map/pallas_call | solution.py:524

commit v3 on v2

--- a/solution.py
+++ b/solution.py
@@ -137,15 +137,15 @@
 
 def kernel(
     doms, snaps,
-    feat, cot, nb, deg, wm, wc, wa, wo,
+    feat, cot, nbt, deg, wm, wc, wa, wo,
     gfeat, wout,
-    ext, cat, oh, oht, wb, slope, comb, spat, spsw, cosw,
+    ext, cat, oh, oht, slope, comb, spat, spsw, cosw,
     q, k, v, ga, gq, gk, gv, att, gsw, gsp, grow, ownf, selff, ghl, ghr,
     part, first_a, second_a, first_b, second_b, first_c, second_c, fin,
     halo_s, halo_r, gho_s, gho_r, cot_s, cot_r, spa_s, spa_r, gra_s, gra_r, *red,
 ):
     local, nodes, width = feat.shape
-    degree = nb.shape[1]
+    degree = nbt.shape[0]
     reach = nodes + 2 * HALO
     share = nodes // snaps
     me_d, me_s = lax.axis_index("dom"), lax.axis_index("snap")
@@ -220,18 +220,18 @@
     ext[:, pl.ds(HALO, nodes), :] = feat[...]
 
     first_row = me_d * nodes - HALO
-    index = nb[...] - first_row
-    index_t = jnp.concatenate([index] * (nodes // degree), axis=1).T
+    index_t = nbt[...] - first_row
+    index = jnp.concatenate([index_t] * (nodes // degree), axis=0).T
     lanes = lax.broadcasted_iota(jnp.int32, (nodes, reach), 1)
     subs = lax.broadcasted_iota(jnp.int32, (reach, nodes), 0)
-    eye = jnp.where(
-        lax.broadcasted_iota(jnp.int32, (nodes, nodes), 0)
-        == lax.broadcasted_iota(jnp.int32, (nodes, nodes), 1),
-        1.0,
-        0.0,
-    ).astype(BF16)
-    counts = jnp.broadcast_to(deg[...], (nodes, nodes)).T
-    inverse = 1.0 / counts.astype(F32)
+    same = lax.broadcasted_iota(jnp.int32, (nodes, nodes), 0) == lax.broadcasted_iota(
+        jnp.int32, (nodes, nodes), 1
+    )
+    one = jnp.where(same, 1.0, 0.0)
+    eye = one.astype(BF16)
+    count_row = deg[...]
+    counts = jnp.broadcast_to(count_row, (nodes, nodes)).T
+    inverse = jnp.concatenate([1.0 / counts.astype(F32)] * (width // nodes), axis=1)
     block = nodes // 2
     for j in range(degree):
         at = pl.ds(j * nodes, nodes)
@@ -240,28 +240,28 @@
             to = pl.ds((c * degree + j) * block, block)
             oh[to, pl.ds(0, reach)] = hit[c * block : (c + 1) * block]
             oh[to, pl.ds(reach, nodes)] = eye[c * block : (c + 1) * block]
-        oht[pl.ds(0, reach), at] = jnp.where(subs == index_t[j : j + 1, :], 1.0, 0.0).astype(BF16)
-        oht[pl.ds(reach, nodes), at] = eye
-        wb[at, :] = jnp.where(counts > j, inverse, 0.0)
+        used = count_row > j
+        row = jnp.where(used, index_t[j : j + 1, :], -1)
+        oht[pl.ds(0, reach), at] = jnp.where(subs == row, 1.0, 0.0).astype(BF16)
+        oht[pl.ds(reach, nodes), at] = jnp.where(used, one, 0.0).astype(BF16)
 
     spa_out = []
     for s in range(local):
         pl.when(has_left)(lambda s=s: to_right(s).wait_recv())
         pl.when(has_right)(lambda s=s: to_left(s).wait_recv())
-        cat[pl.ds(0, reach), :] = dot(ext[s], wm[...]).astype(BF16)
-        cat[pl.ds(reach, nodes), :] = feat[s]
+        cat[pl.ds(0, reach), :] = (0.5 * dot(ext[s], wm[...])).astype(BF16)
+        cat[pl.ds(reach, nodes), :] = (0.5 * feat[s].astype(F32)).astype(BF16)
+        messages = [None] * (degree * nodes // block)
         for c in range(nodes // block):
             before = dot(oh[pl.ds(c * degree * block, degree * block), :], cat[...])
-            total = jnp.zeros((block, width), F32)
             for j in range(degree):
-                at = pl.ds(j * nodes + c * block, block)
-                x = before[j * block : (j + 1) * block]
-                w = jnp.concatenate([wb[at, :]] * halves, axis=1)
-                g = 0.5 * jnp.tanh(0.5 * x) + 0.5
-                y = x * g
-                total = total + w * y
-                slope[s, at, :] = (w * (g + y * (1.0 - g))).astype(BF16)
-            comb[s, pl.ds(c * block, block), :] = total.astype(BF16)
+                half = before[j * block : (j + 1) * block]
+                t = jnp.tanh(half)
+                u = 1.0 + t
+                messages[j * (nodes // block) + c] = (half * u).astype(BF16)
+                slope[s, pl.ds(j * nodes + c * block, block), :] = (u * (1.0 + half * (1.0 - t))).astype(BF16)
+        total = dot(oht[pl.ds(reach, nodes), :], jnp.concatenate(messages))
+        comb[s] = (total * inverse).astype(BF16)
         spat[s] = (feat[s].astype(F32) + dot(comb[s], wc[...])).astype(BF16)
         for d in range(1, snaps):
             p = (me_s + d) % snaps
@@ -390,10 +390,8 @@
     )
     red_b.start()
     for s in range(local):
-        gc = dot_t(gsp[s], wc[...])
-        gb = jnp.concatenate(
-            [(gc * slope[s, pl.ds(j * nodes, nodes), :].astype(F32)).astype(BF16) for j in range(degree)]
-        )
+        gc = (dot_t(gsp[s], wc[...]) * (0.5 * inverse)).astype(BF16)
+        gb = jnp.concatenate([gc * slope[s, pl.ds(j * nodes, nodes), :] for j in range(degree)])
         sums = dot(oht[...], gb)
         grow[s] = sums[:reach].astype(BF16)
         ownf[s] = sums[HALO : HALO + nodes]
@@ -407,15 +405,14 @@
     )
     red_c.start()
     red_b.middle()
-    red_a.spread()
     for s in range(local):
         pl.when(has_right)(lambda s=s: ghost_left(s).wait_recv())
         pl.when(has_left)(lambda s=s: ghost_right(s).wait_recv())
-        if s == local // 2:
-            red_c.middle()
         own = ownf[s] + ghl[s].astype(F32) + ghr[s].astype(F32)
         here = gsp[s].astype(F32) + selff[s] + dot_t(own.astype(BF16), wm[...])
         gfeat[s] = here.astype(BF16)
+    red_c.middle()
+    red_a.spread()
     red_b.spread()
     red_c.spread()
     red_a.finish()
@@ -477,7 +474,6 @@
             vmem((reach + nodes, width), BF16),
             vmem((degree * nodes, reach + nodes), BF16),
             vmem((reach + nodes, degree * nodes), BF16),
-            vmem((degree * nodes, 128), F32),
             vmem((local, degree * nodes, width), BF16),
             vmem((local, nodes, width), BF16),
             vmem((local, nodes, width), BF16),
@@ -516,7 +512,7 @@
             collective_id=0, has_side_effects=True, vmem_limit_bytes=56 * 2**20
         ),
     )(
-        features, cotangent, neighbours, degrees.reshape(1, nodes),
+        features, cotangent, neighbours.T, degrees.reshape(1, nodes),
         message_proj, combine_proj, attend_proj, output_proj,
     )
     factor = 1.0 / math.sqrt(SNAPS * doms * nodes)

time: 61.1 us -> 60.4 us (0.989)
  local copies, waits for them, and re-layouts: 1.43 us -> 0 us
  Pallas kernels: 58.8 us -> 59.6 us
    unnamed x1 -> x0, local copies, waits for them, and re-layouts: 1.43 us -> none
    pallas_call x1, Pallas kernels: 56.3 us -> 57.1 us  [body(): pl.pallas_call(functools.partial(kernel, doms, snaps), out_shape=(jax.Sha...]
where the time goes in v3:
time: 60.4 us; the launch traced here: 60.2 us
  Pallas kernels  59.6 us (99%)
  between operations  0.64 us (1%)
    pallas_call x1, Pallas kernels, body(): pl.pallas_call(functools.partial(kernel, doms, snaps), out_shape=(jax.Sha...  57.1 us
    pallas_call x1, Pallas kernels, body(): pl.pallas_call(functools.partial(finish, factor), out_shape=(jax.ShapeDty...  2.5 us

profile of v3, /device:TPU:11, one launch (start us, length us, event | category | flops | bytes accessed | tf_op | source)
XLA Modules:
  0.0 60.2 jit_solution(9995572625276458977)
XLA Ops:
  0.6 57.1 %shard_map.119 = (bf16[4,128,256]{2,1,0:T(8,128)(2,1)}, bf16[3072,128]{1,0:T(8,128)(2,1)}) custom-call(bf16[4,128,256]{2,1,0:T(8,128)(2,1)} %feat.1, bf16[4,128,256]{2,1,0:T(8,128)(2,1)} %cot.1, s32[16,128]{1,0:T(8,128)} %bitcast.2, s32[1,128]{1,0:T(1,128)} %bitcast.3, bf16[256,256]{1,0:T(8,128)(2,1)} %wm.1, bf16[256,256]{1,0:T(8,128)(2,1)} %wc.1, ...), custom_call_target="tpu_custom_call" | custom-call | tf_op jit(solution)/shard_map/pallas_call | solution.py:464
  57.7 2.5 %shard_map.120 = (bf16[4,128,256]{2,1,0:T(8,128)(2,1)}, f32[256,256]{1,0:T(8,128)}, f32[256,256]{1,0:T(8,128)}, f32[256,768]{1,0:T(8,128)}, f32[256,256]{1,0:T(8,128)}) custom-call(bf16[4,128,256]{2,1,0:T(8,128)(2,1)} %get-tuple-element.7.gfeat, bf16[3072,128]{1,0:T(8,128)(2,1)} %get-tuple-element.8.wout), custom_call_target="tpu_custom_call" | custom-call | tf_op jit(solution)/shard_map/pallas_call | solution.py:520
